TPU v7x, 1024 devices: a whole 4x8x16 slice. The times are simulated.
1024 devices in a mesh: dp: 256 (over y_lo, z, x, core), group: 4 (over y_hi).
Axes of the slice: x: 4, y: 8 (y_hi: 4, y_lo: 2; y = y_hi * 2 + y_lo), z: 16, core: 2. Of those that a mesh axis runs over, the one named last changes fastest.
Arguments:
- image_embed: bfloat16 [131072, 1152], P(('dp', 'group')), may hold values from -6 to 6
- text_embed: bfloat16 [131072, 1152], P(('dp', 'group')), may hold values from -6 to 6
Outputs:
- grad_image: float32 [131072, 1152], P(('dp', 'group'))
- grad_text: float32 [131072, 1152], P(('dp', 'group'))
All inputs are finite; a program needn't handle non-finite values.
Results may differ from a plain program's by a relative error of at most 0.0022.
Values may be sent and summed in bfloat16 or wider, within the bound.
A program may use at most 32 MiB of HBM per device.

v0:
```python
import math

import jax
import jax.numpy as jnp
from jax import lax
from jax.sharding import PartitionSpec as P

HOPS = 4


logit_bias = -2.0


def passed_along(block, axis, distance):
    devices = range(lax.axis_size(axis))
    route = [((i - distance) % len(devices), i) for i in devices]
    return lax.ppermute(block, axis, route)


def pair_terms(images, visiting, labeled):
    scale = 2.0 / math.sqrt(images.shape[1])
    dots = lax.dot_general(
        images, visiting, (((1,), (1,)), ((), ())), preferred_element_type=jnp.float32
    )
    coeff = jax.nn.sigmoid(scale * dots + logit_bias)
    if labeled:
        coeff = coeff - jnp.eye(coeff.shape[0], dtype=jnp.float32)
    coeff = coeff.astype(jnp.bfloat16)
    toward_image = jnp.dot(coeff, visiting, preferred_element_type=jnp.float32)
    toward_text = lax.dot_general(
        coeff, images, (((0,), (0,)), ((), ())), preferred_element_type=jnp.float32
    )
    return (toward_image, toward_text)


def send_back(term, offset):
    return passed_along(term, ("dp", "group"), offset)


def body(image_embed, text_embed):
    scale = 2.0 / math.sqrt(image_embed.shape[1])
    image_sum = jnp.zeros(image_embed.shape, jnp.float32)
    text_sum = jnp.zeros(text_embed.shape, jnp.float32)
    visiting = passed_along(text_embed, ("dp", "group"), -HOPS)
    for step in range(2 * HOPS + 1):
        if step > 0:
            visiting = passed_along(visiting, ("dp", "group"), 1)
        offset = HOPS - step
        toward_image, toward_text = pair_terms(image_embed, visiting, offset == 0)
        image_sum = image_sum + toward_image
        if offset == 0:
            text_sum = text_sum + toward_text
        else:
            text_sum = text_sum + send_back(toward_text, offset)
    return (scale * image_sum, scale * text_sum)


def solution(mesh):
    return jax.shard_map(
        body,
        mesh=mesh,
        in_specs=(P(("dp", "group"), None), P(("dp", "group"), None)),
        out_specs=(P(("dp", "group"), None), P(("dp", "group"), None)),
        check_vma=False,
    )
```

profile of v0, /device:TPU:782, one launch (start us, length us, event | category | flops | bytes accessed | tf_op | source)
XLA Modules:
  0.0 290.1 jit_solution(17049782079987781496)
XLA Ops:
  0.6 0.0 copy-start
  0.6 2.3 collective-permute-start
  3.0 4.5 %collective-permute-done = bf16[128,1152]{1,0:T(8,128)(2,1)S(1)} collective-permute-done((bf16[128,1152]{1,0:T(8,128)(2,1)}, bf16[128,1152]{1,0:T(8,128)(2,1)S(1)}, u32[]{:S(2)}, u32[]{:S(2)}) %collective-permute-start) | collective-permute-done | bytes 294944 | tf_op jit(solution)/shard_map/ppermute | solution.py:17
  7.5 4.5 %collective-permute-start.1 = (bf16[128,1152]{1,0:T(8,128)(2,1)S(1)}, bf16[128,1152]{1,0:T(8,128)(2,1)S(1)}, u32[]{:S(2)}, u32[]{:S(2)}) collective-permute-start(bf16[128,1152]{1,0:T(8,128)(2,1)S(1)} %collective-permute-done), channel_id=1, source_target_pairs={{1023,0},{0,1},{1,2},{2,3},{3,4},{4,5},{5,6},{6,7},{7,8},{8,9},{9,... | collective-permute-start | bytes 884744 | tf_op jit(solution)/shard_map/ppermute | solution.py:17
  12.0 0.0 copy-done
  12.0 0.3 fusion.47
  12.3 0.3 fusion.57
  12.5 5.1 %collective-permute-start.9 = (f32[128,1152]{1,0:T(8,128)S(1)}, f32[128,1152]{1,0:T(8,128)S(1)}, u32[]{:S(2)}, u32[]{:S(2)}) collective-permute-start(f32[128,1152]{1,0:T(8,128)S(1)} %fusion.57), channel_id=1, source_target_pairs={{1020,0},{1021,1},{1022,2},{1023,3},{0,4},{1,5},{2,6},{3,7},{4,8},... | collective-permute-start | bytes 1769480 | tf_op jit(solution)/shard_map/ppermute | solution.py:17
  17.7 0.2 fusion.56
  17.9 9.4 %collective-permute-done.1 = bf16[128,1152]{1,0:T(8,128)(2,1)S(1)} collective-permute-done((bf16[128,1152]{1,0:T(8,128)(2,1)S(1)}, bf16[128,1152]{1,0:T(8,128)(2,1)S(1)}, u32[]{:S(2)}, u32[]{:S(2)}) %collective-permute-start.1) | collective-permute-done | bytes 294944 | tf_op jit(solution)/shard_map/ppermute | solution.py:17
  27.3 0.3 fusion.48
  27.6 3.5 %collective-permute-start.2 = (bf16[128,1152]{1,0:T(8,128)(2,1)S(1)}, bf16[128,1152]{1,0:T(8,128)(2,1)S(1)}, u32[]{:S(2)}, u32[]{:S(2)}) collective-permute-start(bf16[128,1152]{1,0:T(8,128)(2,1)S(1)} %collective-permute-done.1), channel_id=1, source_target_pairs={{1023,0},{0,1},{1,2},{2,3},{3,4},{4,5},{5,6},{6,7},{7,8},{8,9},{9,... | collective-permute-start | bytes 884744 | tf_op jit(solution)/shard_map/ppermute | solution.py:17
  31.1 0.3 fusion.58
  31.3 5.8 %collective-permute-start.10 = (f32[128,1152]{1,0:T(8,128)S(1)}, f32[128,1152]{1,0:T(8,128)S(1)}, u32[]{:S(2)}, u32[]{:S(2)}) collective-permute-start(f32[128,1152]{1,0:T(8,128)S(1)} %fusion.58), channel_id=1, source_target_pairs={{1021,0},{1022,1},{1023,2},{0,3},{1,4},{2,5},{3,6},{4,7},{5,8},{6,... | collective-permute-start | bytes 1769480 | tf_op jit(solution)/shard_map/ppermute | solution.py:17
  37.1 0.2 convolution_add_fusion.7
  37.3 10.1 %collective-permute-done.2 = bf16[128,1152]{1,0:T(8,128)(2,1)S(1)} collective-permute-done((bf16[128,1152]{1,0:T(8,128)(2,1)S(1)}, bf16[128,1152]{1,0:T(8,128)(2,1)S(1)}, u32[]{:S(2)}, u32[]{:S(2)}) %collective-permute-start.2) | collective-permute-done | bytes 294944 | tf_op jit(solution)/shard_map/ppermute | solution.py:17
  47.5 0.3 fusion.49
  47.7 1.9 collective-permute-start.3
  49.7 0.3 fusion.59
  49.9 7.3 %collective-permute-start.11 = (f32[128,1152]{1,0:T(8,128)S(1)}, f32[128,1152]{1,0:T(8,128)S(1)}, u32[]{:S(2)}, u32[]{:S(2)}) collective-permute-start(f32[128,1152]{1,0:T(8,128)S(1)} %fusion.59), channel_id=1, source_target_pairs={{1022,0},{1023,1},{0,2},{1,3},{2,4},{3,5},{4,6},{5,7},{6,8},{7,9},... | collective-permute-start | bytes 1769480 | tf_op jit(solution)/shard_map/ppermute | solution.py:17
  57.3 0.2 convolution_add_fusion.6
  57.5 60.5 %collective-permute-done.3 = bf16[128,1152]{1,0:T(8,128)(2,1)S(1)} collective-permute-done((bf16[128,1152]{1,0:T(8,128)(2,1)S(1)}, bf16[128,1152]{1,0:T(8,128)(2,1)S(1)}, u32[]{:S(2)}, u32[]{:S(2)}) %collective-permute-start.3) | collective-permute-done | bytes 294944 | tf_op jit(solution)/shard_map/ppermute | solution.py:17
  118.0 0.3 fusion.50
  118.3 1.9 collective-permute-start.4
  120.2 0.3 fusion.60
  120.5 13.5 %collective-permute-start.12 = (f32[128,1152]{1,0:T(8,128)S(1)}, f32[128,1152]{1,0:T(8,128)S(1)}, u32[]{:S(2)}, u32[]{:S(2)}) collective-permute-start(f32[128,1152]{1,0:T(8,128)S(1)} %fusion.60), channel_id=1, source_target_pairs={{1023,0},{0,1},{1,2},{2,3},{3,4},{4,5},{5,6},{6,7},{7,8},{8,9},{9,... | collective-permute-start | bytes 1769480 | tf_op jit(solution)/shard_map/ppermute | solution.py:17
  134.0 0.2 convolution_add_fusion.5
  134.2 2.2 collective-permute-done.4
  136.5 9.0 %collective-permute-start.5 = (bf16[128,1152]{1,0:T(8,128)(2,1)S(1)}, bf16[128,1152]{1,0:T(8,128)(2,1)S(1)}, u32[]{:S(2)}, u32[]{:S(2)}) collective-permute-start(bf16[128,1152]{1,0:T(8,128)(2,1)S(1)} %collective-permute-done.4), channel_id=1, source_target_pairs={{1023,0},{0,1},{1,2},{2,3},{3,4},{4,5},{5,6},{6,7},{7,8},{8,9},{9,... | collective-permute-start | bytes 884744 | tf_op jit(solution)/shard_map/ppermute | solution.py:17
  145.4 0.3 fusion.51
  145.7 0.2 convolution_add_fusion.4
  145.9 10.4 %collective-permute-done.5 = bf16[128,1152]{1,0:T(8,128)(2,1)S(1)} collective-permute-done((bf16[128,1152]{1,0:T(8,128)(2,1)S(1)}, bf16[128,1152]{1,0:T(8,128)(2,1)S(1)}, u32[]{:S(2)}, u32[]{:S(2)}) %collective-permute-start.5) | collective-permute-done | bytes 294944 | tf_op jit(solution)/shard_map/ppermute | solution.py:17
  156.4 0.3 fusion.52
  156.6 12.8 %collective-permute-start.6 = (bf16[128,1152]{1,0:T(8,128)(2,1)S(1)}, bf16[128,1152]{1,0:T(8,128)(2,1)S(1)}, u32[]{:S(2)}, u32[]{:S(2)}) collective-permute-start(bf16[128,1152]{1,0:T(8,128)(2,1)S(1)} %collective-permute-done.5), channel_id=1, source_target_pairs={{1023,0},{0,1},{1,2},{2,3},{3,4},{4,5},{5,6},{6,7},{7,8},{8,9},{9,... | collective-permute-start | bytes 884744 | tf_op jit(solution)/shard_map/ppermute | solution.py:17
  169.4 0.3 fusion.61
  169.7 0.2 convolution_add_fusion.3
  169.9 5.2 %collective-permute-done.6 = bf16[128,1152]{1,0:T(8,128)(2,1)S(1)} collective-permute-done((bf16[128,1152]{1,0:T(8,128)(2,1)S(1)}, bf16[128,1152]{1,0:T(8,128)(2,1)S(1)}, u32[]{:S(2)}, u32[]{:S(2)}) %collective-permute-start.6) | collective-permute-done | bytes 294944 | tf_op jit(solution)/shard_map/ppermute | solution.py:17
  175.2 7.9 %collective-permute-start.7 = (bf16[128,1152]{1,0:T(8,128)(2,1)S(1)}, bf16[128,1152]{1,0:T(8,128)(2,1)S(1)}, u32[]{:S(2)}, u32[]{:S(2)}) collective-permute-start(bf16[128,1152]{1,0:T(8,128)(2,1)S(1)} %collective-permute-done.6), channel_id=1, source_target_pairs={{1023,0},{0,1},{1,2},{2,3},{3,4},{4,5},{5,6},{6,7},{7,8},{8,9},{9,... | collective-permute-start | bytes 884744 | tf_op jit(solution)/shard_map/ppermute | solution.py:17
  183.1 0.3 fusion.53
  183.3 0.3 fusion.62
  183.6 9.0 %collective-permute-done.7 = bf16[128,1152]{1,0:T(8,128)(2,1)S(1)} collective-permute-done((bf16[128,1152]{1,0:T(8,128)(2,1)S(1)}, bf16[128,1152]{1,0:T(8,128)(2,1)S(1)}, u32[]{:S(2)}, u32[]{:S(2)}) %collective-permute-start.7) | collective-permute-done | bytes 294944 | tf_op jit(solution)/shard_map/ppermute | solution.py:17
  192.6 5.3 %collective-permute-start.8 = (bf16[128,1152]{1,0:T(8,128)(2,1)S(1)}, bf16[128,1152]{1,0:T(8,128)(2,1)S(1)}, u32[]{:S(2)}, u32[]{:S(2)}) collective-permute-start(bf16[128,1152]{1,0:T(8,128)(2,1)S(1)} %collective-permute-done.7), channel_id=1, source_target_pairs={{1023,0},{0,1},{1,2},{2,3},{3,4},{4,5},{5,6},{6,7},{7,8},{8,9},{9,... | collective-permute-start | bytes 884744 | tf_op jit(solution)/shard_map/ppermute | solution.py:17
  197.9 0.3 fusion.54
  198.2 0.3 fusion.63
  198.5 43.3 %collective-permute-done.8 = bf16[128,1152]{1,0:T(8,128)(2,1)S(1)} collective-permute-done((bf16[128,1152]{1,0:T(8,128)(2,1)S(1)}, bf16[128,1152]{1,0:T(8,128)(2,1)S(1)}, u32[]{:S(2)}, u32[]{:S(2)}) %collective-permute-start.8) | collective-permute-done | bytes 294944 | tf_op jit(solution)/shard_map/ppermute | solution.py:17
  241.8 1.9 collective-permute-start.13
  243.7 0.3 fusion.55
  243.9 0.3 fusion.64
  244.2 0.0 collective-permute-done.9
  244.2 1.9 collective-permute-start.14
  246.1 0.0 collective-permute-done.10
  246.2 1.9 collective-permute-start.15
  248.1 0.0 collective-permute-done.11
  248.1 7.3 %collective-permute-start.16 = (f32[128,1152]{1,0:T(8,128)S(1)}, f32[128,1152]{1,0:T(8,128)S(1)}, u32[]{:S(2)}, u32[]{:S(2)}) collective-permute-start(f32[128,1152]{1,0:T(8,128)S(1)} %fusion.64), channel_id=1, source_target_pairs={{4,0},{5,1},{6,2},{7,3},{8,4},{9,5},{10,6},{11,7},{12,8},{13,9},{1... | collective-permute-start | bytes 1769480 | tf_op jit(solution)/shard_map/ppermute | solution.py:17
  255.4 0.2 convolution_add_fusion.2
  255.7 0.2 convolution_add_fusion.1
  255.9 1.0 fusion
  256.9 0.0 collective-permute-done.12
  256.9 4.0 %collective-permute-done.13 = f32[128,1152]{1,0:T(8,128)S(1)} collective-permute-done((f32[128,1152]{1,0:T(8,128)S(1)}, f32[128,1152]{1,0:T(8,128)S(1)}, u32[]{:S(2)}, u32[]{:S(2)}) %collective-permute-start.13) | collective-permute-done | bytes 589856 | tf_op jit(solution)/shard_map/ppermute | solution.py:17
  260.9 28.0 %collective-permute-done.14 = f32[128,1152]{1,0:T(8,128)S(1)} collective-permute-done((f32[128,1152]{1,0:T(8,128)S(1)}, f32[128,1152]{1,0:T(8,128)S(1)}, u32[]{:S(2)}, u32[]{:S(2)}) %collective-permute-start.14) | collective-permute-done | bytes 589856 | tf_op jit(solution)/shard_map/ppermute | solution.py:17
  288.9 0.0 collective-permute-done.15
  288.9 0.0 collective-permute-done.16
  288.9 1.2 add_multiply_fusion
Async XLA Ops:
  0.6 11.4 %copy-start = (bf16[128,1152]{1,0:T(8,128)(2,1)S(1)}, bf16[128,1152]{1,0:T(8,128)(2,1)}, u32[]{:S(2)}) copy-start(bf16[128,1152]{1,0:T(8,128)(2,1)} %param.2) | copy-start | bytes 884740
  0.6 6.9 %collective-permute-start = (bf16[128,1152]{1,0:T(8,128)(2,1)}, bf16[128,1152]{1,0:T(8,128)(2,1)S(1)}, u32[]{:S(2)}, u32[]{:S(2)}) collective-permute-start(bf16[128,1152]{1,0:T(8,128)(2,1)} %param.3), channel_id=1, source_target_pairs={{4,0},{5,1},{6,2},{7,3},{8,4},{9,5},{10,6},{11,7},{12,8},{13,9},{1... | collective-permute-start | bytes 884744 | tf_op jit(solution)/shard_map/ppermute | solution.py:17
  7.5 19.8 %collective-permute-start.1 = (bf16[128,1152]{1,0:T(8,128)(2,1)S(1)}, bf16[128,1152]{1,0:T(8,128)(2,1)S(1)}, u32[]{:S(2)}, u32[]{:S(2)}) collective-permute-start(bf16[128,1152]{1,0:T(8,128)(2,1)S(1)} %collective-permute-done), channel_id=1, source_target_pairs={{1023,0},{0,1},{1,2},{2,3},{3,4},{4,5},{5,6},{6,7},{7,8},{8,9},{9,... | collective-permute-start | bytes 884744 | tf_op jit(solution)/shard_map/ppermute | solution.py:17
  12.5 231.7 %collective-permute-start.9 = (f32[128,1152]{1,0:T(8,128)S(1)}, f32[128,1152]{1,0:T(8,128)S(1)}, u32[]{:S(2)}, u32[]{:S(2)}) collective-permute-start(f32[128,1152]{1,0:T(8,128)S(1)} %fusion.57), channel_id=1, source_target_pairs={{1020,0},{1021,1},{1022,2},{1023,3},{0,4},{1,5},{2,6},{3,7},{4,8},... | collective-permute-start | bytes 1769480 | tf_op jit(solution)/shard_map/ppermute | solution.py:17
  27.6 19.9 %collective-permute-start.2 = (bf16[128,1152]{1,0:T(8,128)(2,1)S(1)}, bf16[128,1152]{1,0:T(8,128)(2,1)S(1)}, u32[]{:S(2)}, u32[]{:S(2)}) collective-permute-start(bf16[128,1152]{1,0:T(8,128)(2,1)S(1)} %collective-permute-done.1), channel_id=1, source_target_pairs={{1023,0},{0,1},{1,2},{2,3},{3,4},{4,5},{5,6},{6,7},{7,8},{8,9},{9,... | collective-permute-start | bytes 884744 | tf_op jit(solution)/shard_map/ppermute | solution.py:17
  31.3 214.8 %collective-permute-start.10 = (f32[128,1152]{1,0:T(8,128)S(1)}, f32[128,1152]{1,0:T(8,128)S(1)}, u32[]{:S(2)}, u32[]{:S(2)}) collective-permute-start(f32[128,1152]{1,0:T(8,128)S(1)} %fusion.58), channel_id=1, source_target_pairs={{1021,0},{1022,1},{1023,2},{0,3},{1,4},{2,5},{3,6},{4,7},{5,8},{6,... | collective-permute-start | bytes 1769480 | tf_op jit(solution)/shard_map/ppermute | solution.py:17
  47.7 70.3 %collective-permute-start.3 = (bf16[128,1152]{1,0:T(8,128)(2,1)S(1)}, bf16[128,1152]{1,0:T(8,128)(2,1)S(1)}, u32[]{:S(2)}, u32[]{:S(2)}) collective-permute-start(bf16[128,1152]{1,0:T(8,128)(2,1)S(1)} %collective-permute-done.2), channel_id=1, source_target_pairs={{1023,0},{0,1},{1,2},{2,3},{3,4},{4,5},{5,6},{6,7},{7,8},{8,9},{9,... | collective-permute-start | bytes 884744 | tf_op jit(solution)/shard_map/ppermute | solution.py:17
  49.9 198.2 %collective-permute-start.11 = (f32[128,1152]{1,0:T(8,128)S(1)}, f32[128,1152]{1,0:T(8,128)S(1)}, u32[]{:S(2)}, u32[]{:S(2)}) collective-permute-start(f32[128,1152]{1,0:T(8,128)S(1)} %fusion.59), channel_id=1, source_target_pairs={{1022,0},{1023,1},{0,2},{1,3},{2,4},{3,5},{4,6},{5,7},{6,8},{7,9},... | collective-permute-start | bytes 1769480 | tf_op jit(solution)/shard_map/ppermute | solution.py:17
  118.3 18.2 %collective-permute-start.4 = (bf16[128,1152]{1,0:T(8,128)(2,1)S(1)}, bf16[128,1152]{1,0:T(8,128)(2,1)S(1)}, u32[]{:S(2)}, u32[]{:S(2)}) collective-permute-start(bf16[128,1152]{1,0:T(8,128)(2,1)S(1)} %collective-permute-done.3), channel_id=1, source_target_pairs={{1023,0},{0,1},{1,2},{2,3},{3,4},{4,5},{5,6},{6,7},{7,8},{8,9},{9,... | collective-permute-start | bytes 884744 | tf_op jit(solution)/shard_map/ppermute | solution.py:17
  120.5 136.5 %collective-permute-start.12 = (f32[128,1152]{1,0:T(8,128)S(1)}, f32[128,1152]{1,0:T(8,128)S(1)}, u32[]{:S(2)}, u32[]{:S(2)}) collective-permute-start(f32[128,1152]{1,0:T(8,128)S(1)} %fusion.60), channel_id=1, source_target_pairs={{1023,0},{0,1},{1,2},{2,3},{3,4},{4,5},{5,6},{6,7},{7,8},{8,9},{9,... | collective-permute-start | bytes 1769480 | tf_op jit(solution)/shard_map/ppermute | solution.py:17
  136.5 19.9 %collective-permute-start.5 = (bf16[128,1152]{1,0:T(8,128)(2,1)S(1)}, bf16[128,1152]{1,0:T(8,128)(2,1)S(1)}, u32[]{:S(2)}, u32[]{:S(2)}) collective-permute-start(bf16[128,1152]{1,0:T(8,128)(2,1)S(1)} %collective-permute-done.4), channel_id=1, source_target_pairs={{1023,0},{0,1},{1,2},{2,3},{3,4},{4,5},{5,6},{6,7},{7,8},{8,9},{9,... | collective-permute-start | bytes 884744 | tf_op jit(solution)/shard_map/ppermute | solution.py:17
  156.6 18.5 %collective-permute-start.6 = (bf16[128,1152]{1,0:T(8,128)(2,1)S(1)}, bf16[128,1152]{1,0:T(8,128)(2,1)S(1)}, u32[]{:S(2)}, u32[]{:S(2)}) collective-permute-start(bf16[128,1152]{1,0:T(8,128)(2,1)S(1)} %collective-permute-done.5), channel_id=1, source_target_pairs={{1023,0},{0,1},{1,2},{2,3},{3,4},{4,5},{5,6},{6,7},{7,8},{8,9},{9,... | collective-permute-start | bytes 884744 | tf_op jit(solution)/shard_map/ppermute | solution.py:17
  175.2 17.4 %collective-permute-start.7 = (bf16[128,1152]{1,0:T(8,128)(2,1)S(1)}, bf16[128,1152]{1,0:T(8,128)(2,1)S(1)}, u32[]{:S(2)}, u32[]{:S(2)}) collective-permute-start(bf16[128,1152]{1,0:T(8,128)(2,1)S(1)} %collective-permute-done.6), channel_id=1, source_target_pairs={{1023,0},{0,1},{1,2},{2,3},{3,4},{4,5},{5,6},{6,7},{7,8},{8,9},{9,... | collective-permute-start | bytes 884744 | tf_op jit(solution)/shard_map/ppermute | solution.py:17
  192.6 49.1 %collective-permute-start.8 = (bf16[128,1152]{1,0:T(8,128)(2,1)S(1)}, bf16[128,1152]{1,0:T(8,128)(2,1)S(1)}, u32[]{:S(2)}, u32[]{:S(2)}) collective-permute-start(bf16[128,1152]{1,0:T(8,128)(2,1)S(1)} %collective-permute-done.7), channel_id=1, source_target_pairs={{1023,0},{0,1},{1,2},{2,3},{3,4},{4,5},{5,6},{6,7},{7,8},{8,9},{9,... | collective-permute-start | bytes 884744 | tf_op jit(solution)/shard_map/ppermute | solution.py:17
  241.8 19.2 %collective-permute-start.13 = (f32[128,1152]{1,0:T(8,128)S(1)}, f32[128,1152]{1,0:T(8,128)S(1)}, u32[]{:S(2)}, u32[]{:S(2)}) collective-permute-start(f32[128,1152]{1,0:T(8,128)S(1)} %fusion.61), channel_id=1, source_target_pairs={{1,0},{2,1},{3,2},{4,3},{5,4},{6,5},{7,6},{8,7},{9,8},{10,9},{11,1... | collective-permute-start | bytes 1769480 | tf_op jit(solution)/shard_map/ppermute | solution.py:17
  244.2 44.7 %collective-permute-start.14 = (f32[128,1152]{1,0:T(8,128)S(1)}, f32[128,1152]{1,0:T(8,128)S(1)}, u32[]{:S(2)}, u32[]{:S(2)}) collective-permute-start(f32[128,1152]{1,0:T(8,128)S(1)} %fusion.62), channel_id=1, source_target_pairs={{2,0},{3,1},{4,2},{5,3},{6,4},{7,5},{8,6},{9,7},{10,8},{11,9},{12,... | collective-permute-start | bytes 1769480 | tf_op jit(solution)/shard_map/ppermute | solution.py:17
  246.2 42.7 %collective-permute-start.15 = (f32[128,1152]{1,0:T(8,128)S(1)}, f32[128,1152]{1,0:T(8,128)S(1)}, u32[]{:S(2)}, u32[]{:S(2)}) collective-permute-start(f32[128,1152]{1,0:T(8,128)S(1)} %fusion.63), channel_id=1, source_target_pairs={{3,0},{4,1},{5,2},{6,3},{7,4},{8,5},{9,6},{10,7},{11,8},{12,9},{13... | collective-permute-start | bytes 1769480 | tf_op jit(solution)/shard_map/ppermute | solution.py:17
  248.1 40.8 %collective-permute-start.16 = (f32[128,1152]{1,0:T(8,128)S(1)}, f32[128,1152]{1,0:T(8,128)S(1)}, u32[]{:S(2)}, u32[]{:S(2)}) collective-permute-start(f32[128,1152]{1,0:T(8,128)S(1)} %fusion.64), channel_id=1, source_target_pairs={{4,0},{5,1},{6,2},{7,3},{8,4},{9,5},{10,6},{11,7},{12,8},{13,9},{1... | collective-permute-start | bytes 1769480 | tf_op jit(solution)/shard_map/ppermute | solution.py:17
where the time goes:
time: 291 us; the launch traced here: 290 us
  waiting for transfers between devices  187 us (64%)
  starting transfers between devices  93.9 us (32%)
  matrix products  8.48 us (3%)
    ppermute x17, waiting for transfers between devices, passed_along(): return lax.ppermute(block, axis, route)  187 us
    ppermute x17, starting transfers between devices, passed_along(): return lax.ppermute(block, axis, route)  93.9 us
  transfers between devices with their start and end apart: 17, of which 11 were waited for; matrix products, arithmetic and copies ran while one was open for 3% of the time, Pallas kernels for 0%

commit v1 on v0

v1 whole, which is shorter than its diff:
```python
import math

import jax
import jax.numpy as jnp
from jax import lax
from jax.experimental import pallas as pl
from jax.experimental.pallas import tpu as pltpu
from jax.sharding import PartitionSpec as P

MESH = pl.DeviceIdType.MESH
BIAS = -2.0
ROWS = 128
CHUNKS = 4
STEP = ROWS // CHUNKS
TILE = 384

HERE, PARTNER, UP, UP_PARTNER, DOWN, DOWN_PARTNER = range(6)


def block(i):
    return pl.ds(i * ROWS, ROWS)


def part(i, k):
    return pl.ds(i * ROWS + k * STEP, STEP)


def kernel(image_ref, text_ref, grad_image_ref, grad_text_ref, images, texts, coeffs, leaving, arriving, send_sem, recv_sem, local_sem):
    h, g = lax.axis_index("dp"), lax.axis_index("group")
    n = lax.axis_size("dp")
    row_g, col_g = g ^ 1, 3 - g
    row, col = (h, row_g), (h, col_g)
    up, down = (lax.rem(h + 1, n), g), (lax.rem(h + n - 1, n), g)
    scale = 2.0 / math.sqrt(image_ref.shape[1])

    loads = [
        pltpu.make_async_copy(image_ref, images.at[block(HERE)], local_sem.at[0]),
        pltpu.make_async_copy(text_ref, texts.at[block(HERE)], local_sem.at[1]),
    ]
    for load in loads:
        load.start()

    barrier = pltpu.get_barrier_semaphore()
    for other in (row, col, up, down):
        pl.semaphore_signal(barrier, inc=1, device_id=other, device_id_type=MESH)

    image_up, image_down = g != 2, g != 1
    text_up, text_down = g >= 2, g < 2
    zero = jnp.zeros((ROWS, images.shape[1]), images.dtype)
    for needed, buf, slot in (
        (image_up, images, UP_PARTNER),
        (image_down, images, DOWN_PARTNER),
        (text_up, texts, UP_PARTNER),
        (text_down, texts, DOWN_PARTNER),
    ):

        @pl.when(jnp.logical_not(needed))
        def _(buf=buf, slot=slot):
            buf[block(slot), :] = zero

    for load in loads:
        load.wait()
    pl.semaphore_wait(barrier, 4)

    count = [0]

    def copy(src, dst, device):
        i = count[0]
        count[0] += 1
        return pltpu.make_async_remote_copy(
            src_ref=src, dst_ref=dst, send_sem=send_sem.at[i], recv_sem=recv_sem.at[i], device_id=device, device_id_type=MESH
        )

    def sent(buf, frm, to, device, k):
        return copy(buf.at[part(frm, k)], buf.at[part(to, k)], device)

    imports = [(sent(images, HERE, PARTNER, row, k), sent(texts, HERE, PARTNER, col, k)) for k in range(CHUNKS)]
    shares = [
        copy(buf.at[block(HERE)], buf.at[block(to)], device)
        for to, device in ((DOWN, up), (UP, down))
        for buf in (images, texts)
    ]
    forwards = [
        (
            (image_down, sent(images, PARTNER, DOWN_PARTNER, up, k)),
            (image_up, sent(images, PARTNER, UP_PARTNER, down, k)),
            (text_down, sent(texts, PARTNER, DOWN_PARTNER, up, k)),
            (text_up, sent(texts, PARTNER, UP_PARTNER, down, k)),
        )
        for k in range(CHUNKS)
    ]
    returns = [
        [copy(leaving.at[part(s, k)], arriving.at[part(s, k)], device) for k in range(CHUNKS)]
        for s, device in ((0, row), (1, col))
    ]

    for pair in imports:
        for c in pair:
            c.start()
    for c in shares:
        c.start()
    for k in range(CHUNKS):
        image_in, text_in = imports[k]
        fwd = forwards[k]
        image_in.wait_recv()
        for needed, c in fwd[:2]:
            pl.when(needed)(c.start)
        text_in.wait_recv()
        for needed, c in fwd[2:]:
            pl.when(needed)(c.start)

    eye = (
        lax.broadcasted_iota(jnp.int32, (ROWS, ROWS), 0) == lax.broadcasted_iota(jnp.int32, (ROWS, ROWS), 1)
    ).astype(jnp.float32)

    def fill(side, mine, others, first, last):
        my_g = (g, row_g) if side == 0 else (g, col_g)
        other_g = (g, col_g) if side == 0 else (g, row_g)
        for a in range(2):
            dots = lax.dot_general(
                mine[block(a), :],
                others[pl.ds(first * ROWS, (last - first) * ROWS), :],
                (((1,), (1,)), ((), ())),
                preferred_element_type=jnp.float32,
            )
            value = jax.nn.sigmoid(scale * dots + BIAS)
            for j in range(first, last):
                piece = value[:, (j - first) * ROWS : (j - first + 1) * ROWS]
                if j == HERE and a == 0:
                    piece = piece - eye
                if j >= UP:
                    ahead, behind = my_g[a] >= other_g[j % 2], my_g[a] <= other_g[j % 2]
                    valid = ahead if j < DOWN else behind
                    piece = piece * jnp.where(valid, 1.0, 0.0)
                coeffs[side, block(a), block(j)] = piece.astype(jnp.bfloat16)

    sides = ((0, images, texts), (1, texts, images))
    for s, mine, others in sides:
        fill(s, mine, others, HERE, UP)
    for c in shares:
        c.wait_recv()
    for k in range(CHUNKS):
        for needed, c in forwards[k]:
            pl.when(needed)(c.wait_recv)
    for s, mine, others in sides:
        fill(s, mine, others, UP, DOWN_PARTNER + 1)

    width = images.shape[1]
    for s, mine, others in sides:
        for t in range(0, width, TILE):
            leaving[block(s), t : t + TILE] = jnp.dot(
                coeffs[s, block(1), :], others[:, t : t + TILE], preferred_element_type=jnp.float32
            ).astype(jnp.bfloat16)
        for c in returns[s]:
            c.start()
    outs = (grad_image_ref, grad_text_ref)
    for s, mine, others in sides:
        for t in range(0, width, TILE):
            outs[s][:, t : t + TILE] = jnp.dot(
                coeffs[s, block(0), :], others[:, t : t + TILE], preferred_element_type=jnp.float32
            )
    for k in range(CHUNKS):
        for s in range(2):
            returns[s][k].wait_recv()
            at = pl.ds(k * STEP, STEP)
            outs[s][at, :] = scale * (outs[s][at, :] + arriving[part(s, k), :].astype(jnp.float32))

    for pair in imports:
        for c in pair:
            c.wait_send()
    for c in shares:
        c.wait_send()
    for fwd in forwards:
        for needed, c in fwd:
            pl.when(needed)(c.wait_send)
    for side in returns:
        for c in side:
            c.wait_send()


def body(image_embed, text_embed):
    rows, width = image_embed.shape
    copies = 2 * CHUNKS + 4 + 4 * CHUNKS + 2 * CHUNKS
    return pl.pallas_call(
        kernel,
        out_shape=[jax.ShapeDtypeStruct((rows, width), jnp.float32)] * 2,
        in_specs=[pl.BlockSpec(memory_space=pl.ANY)] * 2,
        out_specs=[pl.BlockSpec(memory_space=pltpu.VMEM)] * 2,
        scratch_shapes=[
            pltpu.VMEM((6 * rows, width), jnp.bfloat16),
            pltpu.VMEM((6 * rows, width), jnp.bfloat16),
            pltpu.VMEM((2, 2 * rows, 6 * rows), jnp.bfloat16),
            pltpu.VMEM((2 * rows, width), jnp.bfloat16),
            pltpu.VMEM((2 * rows, width), jnp.bfloat16),
            pltpu.SemaphoreType.DMA((copies,)),
            pltpu.SemaphoreType.DMA((copies,)),
            pltpu.SemaphoreType.DMA((2,)),
        ],
        compiler_params=pltpu.CompilerParams(
            collective_id=0, has_side_effects=True, vmem_limit_bytes=48 * 1024 * 1024
        ),
        cost_estimate=pl.CostEstimate(flops=2 * 4 * 256 * 768 * 1152, bytes_accessed=6 * rows * width * 2, transcendentals=2 * 256 * 768),
    )(image_embed, text_embed)


def solution(mesh):
    spec = P(("dp", "group"), None)
    return jax.shard_map(body, mesh=mesh, in_specs=(spec, spec), out_specs=(spec, spec), check_vma=False)
```

time: 291 us -> 57.3 us (0.20)
  the two profiles are of different devices: /device:TPU:782 before, /device:TPU:24 now
where the time goes in v1:
time: 57.3 us; the launch traced here: 57.1 us
  Pallas kernels  52.9 us (92%)
  local copies, waits for them, and re-layouts  3.55 us (6%)
  between operations  0.65 us (1%)
    pallas_call x1, Pallas kernels, body(): pl.pallas_call(kernel, out_shape=[jax.ShapeDtypeStruct((rows, width), jnp...  52.9 us
    unnamed x6, local copies, waits for them, and re-layouts  3.55 us

profile of v1, /device:TPU:24, one launch (start us, length us, event | category | flops | bytes accessed | tf_op | source)
XLA Modules:
  0.0 57.1 jit_solution(232006506780789225)
XLA Ops:
  0.6 0.0 copy-start
  0.6 1.0 %copy-done = bf16[128,1152]{1,0:T(8,128)(2,1)S(1)} copy-done((bf16[128,1152]{1,0:T(8,128)(2,1)S(1)}, bf16[128,1152]{1,0:T(8,128)(2,1)}, u32[]{:S(2)}) %copy-start) | copy-done | bytes 294936
  1.6 0.0 copy-start.1
  1.6 1.0 %copy-done.1 = bf16[128,1152]{1,0:T(8,128)(2,1)S(1)} copy-done((bf16[128,1152]{1,0:T(8,128)(2,1)S(1)}, bf16[128,1152]{1,0:T(8,128)(2,1)}, u32[]{:S(2)}) %copy-start.1) | copy-done | bytes 294936
  2.6 52.9 %shard_map.41 = (f32[128,1152]{1,0:T(8,128)S(1)}, f32[128,1152]{1,0:T(8,128)S(1)}) custom-call(bf16[128,1152]{1,0:T(8,128)(2,1)S(1)} %copy-done, bf16[128,1152]{1,0:T(8,128)(2,1)S(1)} %copy-done.1), custom_call_target="tpu_custom_call" | custom-call | flops 1811939328 | bytes 1769472 | tf_op jit(solution)/shard_map/pallas_call | solution.py:184
  55.5 0.8 %copy.6 = f32[128,1152]{1,0:T(8,128)} copy(f32[128,1152]{1,0:T(8,128)S(1)} %get-tuple-element.4) | data formatting | bytes 1179648
  56.3 0.8 %copy.7 = f32[128,1152]{1,0:T(8,128)} copy(f32[128,1152]{1,0:T(8,128)S(1)} %get-tuple-element.5) | data formatting | bytes 1179648
Async XLA Ops:
  0.6 1.0 %copy-start = (bf16[128,1152]{1,0:T(8,128)(2,1)S(1)}, bf16[128,1152]{1,0:T(8,128)(2,1)}, u32[]{:S(2)}) copy-start(bf16[128,1152]{1,0:T(8,128)(2,1)} %image_ref.1) | copy-start | bytes 884740
  1.6 1.0 %copy-start.1 = (bf16[128,1152]{1,0:T(8,128)(2,1)S(1)}, bf16[128,1152]{1,0:T(8,128)(2,1)}, u32[]{:S(2)}) copy-start(bf16[128,1152]{1,0:T(8,128)(2,1)} %text_ref.1) | copy-start | bytes 884740

commit v2 on v1

v2 whole, which is shorter than its diff:
```python
import math

import jax
import jax.numpy as jnp
from jax import lax
from jax.experimental import pallas as pl
from jax.experimental.pallas import tpu as pltpu
from jax.sharding import PartitionSpec as P

MESH = pl.DeviceIdType.MESH
BIAS = -2.0
ROWS = 128
CHUNKS = 4
STEP = ROWS // CHUNKS
TILE = 384
VMEM_BYTES = 64 * 1024 * 1024

HERE, PARTNER, UP, UP_PARTNER, DOWN, DOWN_PARTNER = range(6)

PLANES = 2


def block(i):
    return pl.ds(pl.multiple_of(i * ROWS, ROWS), ROWS)


def part(i, k):
    return pl.ds(pl.multiple_of(i * ROWS + k * STEP, STEP), STEP)


def kernel(image_ref, text_ref, own_image_ref, own_text_ref, arriving, images, texts, coeffs, leaving, own, send_sem, recv_sem, local_sem):
    h, g = lax.axis_index("dp"), lax.axis_index("group")
    n = lax.axis_size("dp")
    plane = n // PLANES
    place = h % plane
    row_g, col_g = g ^ 1, 3 - g
    row, col = (h, row_g), (h, col_g)
    up, down = ((h + 1) % n, g), ((h + n - 1) % n, g)
    across_h = jnp.where(place == 0, h + n - 1, h + 1) % n
    across_row, across_col = (across_h, row_g), (across_h, col_g)
    first, last = place == 0, place == plane - 1
    edge = jnp.logical_or(first, last)
    scale = 2.0 / math.sqrt(image_ref.shape[1])

    loads = [
        pltpu.make_async_copy(image_ref, images.at[block(HERE)], local_sem.at[0]),
        pltpu.make_async_copy(text_ref, texts.at[block(HERE)], local_sem.at[1]),
    ]
    for load in loads:
        load.start()

    barrier = pltpu.get_barrier_semaphore()

    def greet(*others):
        for other in others:
            pl.semaphore_signal(barrier, inc=1, device_id=other, device_id_type=MESH)

    greet(row, col, up, down)
    pl.when(edge)(lambda: greet(across_row, across_col))

    image_up, image_down = g != 2, g != 1
    text_up, text_down = g >= 2, g < 2
    zero = jnp.zeros((ROWS, images.shape[1]), images.dtype)
    for needed, buf, slot in (
        (image_up, images, UP_PARTNER),
        (image_down, images, DOWN_PARTNER),
        (text_up, texts, UP_PARTNER),
        (text_down, texts, DOWN_PARTNER),
    ):

        @pl.when(jnp.logical_not(needed))
        def _(buf=buf, slot=slot):
            buf[block(slot), :] = zero

    for load in loads:
        load.wait()
    pl.semaphore_wait(barrier, jnp.where(edge, 6, 4))

    count = [0]

    def copy(src, dst, device):
        i = count[0]
        count[0] += 1
        return pltpu.make_async_remote_copy(
            src_ref=src, dst_ref=dst, send_sem=send_sem.at[i], recv_sem=recv_sem.at[i], device_id=device, device_id_type=MESH
        )

    def whole(buf, frm, to, device):
        return copy(buf.at[block(frm)], buf.at[block(to)], device)

    def piece(buf, frm, to, device, k):
        return copy(buf.at[part(frm, k)], buf.at[part(to, k)], device)

    every = range(CHUNKS)
    both = (images, texts)
    imports = [(piece(images, HERE, PARTNER, row, k), piece(texts, HERE, PARTNER, col, k)) for k in every]
    share_up = [(True, whole(buf, HERE, DOWN, up)) for buf in both]
    share_down = [(True, whole(buf, HERE, UP, down)) for buf in both]
    forward_up = [
        [(needed, piece(buf, PARTNER, DOWN_PARTNER, up, k)) for needed, buf in ((image_down, images), (text_down, texts))]
        for k in every
    ]
    forward_down = [
        [(needed, piece(buf, PARTNER, UP_PARTNER, down, k)) for needed, buf in ((image_up, images), (text_up, texts))]
        for k in every
    ]
    across = [whole(images, HERE, DOWN_PARTNER, across_row), whole(texts, HERE, DOWN_PARTNER, across_col)]
    across_out = list(zip((row_g != 1, col_g < 2), across))
    across_in = list(zip((image_down, text_down), across))
    returns = [
        [(True, copy(leaving.at[part(s, k)], arriving.at[part(s, k)], device)) for k in every] for s, device in ((0, row), (1, col))
    ]

    def each(method, *lists):
        for copies in lists:
            for needed, c in copies:
                if needed is True:
                    getattr(c, method)()
                else:
                    pl.when(needed)(getattr(c, method))

    pl.when(last)(lambda: each("start", share_up, across_out))
    for pair in imports:
        for c in pair:
            c.start()
    pl.when(jnp.logical_not(last))(lambda: each("start", share_up))
    each("start", share_down)
    for k in every:
        for i in range(2):
            imports[k][i].wait_recv()
            pl.when(jnp.logical_not(last))(lambda k=k, i=i: each("start", forward_up[k][i : i + 1]))
            each("start", forward_down[k][i : i + 1])

    eye = (
        lax.broadcasted_iota(jnp.int32, (ROWS, ROWS), 0) == lax.broadcasted_iota(jnp.int32, (ROWS, ROWS), 1)
    ).astype(jnp.float32)

    def fill(side, mine, others, begin, end):
        my_g = (g, row_g) if side == 0 else (g, col_g)
        other_g = (g, col_g) if side == 0 else (g, row_g)
        for a in range(2):
            dots = lax.dot_general(
                mine[block(a), :],
                others[begin * ROWS : end * ROWS, :],
                (((1,), (1,)), ((), ())),
                preferred_element_type=jnp.float32,
            )
            value = jax.nn.sigmoid(scale * dots + BIAS)
            for j in range(begin, end):
                some = value[:, (j - begin) * ROWS : (j - begin + 1) * ROWS]
                if j == HERE and a == 0:
                    some = some - eye
                if j >= UP:
                    ahead, behind = my_g[a] >= other_g[j % 2], my_g[a] <= other_g[j % 2]
                    valid = ahead if j < DOWN else behind
                    some = some * jnp.where(valid, 1.0, 0.0)
                coeffs[side, block(a), block(j)] = some.astype(jnp.bfloat16)

    sides = ((0, images, texts), (1, texts, images))
    for s, mine, others in sides:
        fill(s, mine, others, HERE, UP)

    each("wait_recv", share_down, *forward_down)
    for s, mine, others in sides:
        fill(s, mine, others, UP, DOWN)

    each("wait_recv", share_up)
    pl.when(first)(lambda: each("wait_recv", across_in))
    pl.when(jnp.logical_not(first))(lambda: each("wait_recv", *forward_up))

    width = images.shape[1]
    worked = (DOWN_PARTNER + 1) * ROWS
    stores = [pltpu.make_async_copy(own.at[s], ref, local_sem.at[s]) for s, ref in enumerate((own_image_ref, own_text_ref))]
    for s, mine, others in sides:
        fill(s, mine, others, DOWN, DOWN_PARTNER + 1)
        for t in range(0, width, TILE):
            leaving[block(s), t : t + TILE] = jnp.dot(
                coeffs[s, block(1), :], others[:worked, t : t + TILE], preferred_element_type=jnp.float32
            ).astype(jnp.bfloat16)
        each("start", returns[s])
    for s, mine, others in sides:
        for t in range(0, width, TILE):
            own[s, :, t : t + TILE] = jnp.dot(
                coeffs[s, block(0), :], others[:worked, t : t + TILE], preferred_element_type=jnp.float32
            )
        stores[s].start()
    for store in stores:
        store.wait()
    each("wait_recv", *returns)

    for pair in imports:
        for c in pair:
            c.wait_send()
    each("wait_send", share_up, share_down, *forward_down, *returns)
    pl.when(last)(lambda: each("wait_send", across_out))
    pl.when(jnp.logical_not(last))(lambda: each("wait_send", *forward_up))


def body(image_embed, text_embed):
    rows, width = image_embed.shape
    copies = 8 * CHUNKS + 6
    own_image, own_text, arrived = pl.pallas_call(
        kernel,
        out_shape=[jax.ShapeDtypeStruct((rows, width), jnp.float32)] * 2 + [jax.ShapeDtypeStruct((2 * rows, width), jnp.bfloat16)],
        in_specs=[pl.BlockSpec(memory_space=pl.ANY)] * 2,
        out_specs=[pl.BlockSpec(memory_space=pl.ANY)] * 3,
        scratch_shapes=[
            pltpu.VMEM((6 * rows, width), jnp.bfloat16),
            pltpu.VMEM((6 * rows, width), jnp.bfloat16),
            pltpu.VMEM((2, 2 * rows, 6 * rows), jnp.bfloat16),
            pltpu.VMEM((2 * rows, width), jnp.bfloat16),
            pltpu.VMEM((2, rows, width), jnp.float32),
            pltpu.SemaphoreType.DMA((copies,)),
            pltpu.SemaphoreType.DMA((copies,)),
            pltpu.SemaphoreType.DMA((2,)),
        ],
        compiler_params=pltpu.CompilerParams(collective_id=0, has_side_effects=True, vmem_limit_bytes=VMEM_BYTES),
    )(image_embed, text_embed)
    scale = 2.0 / math.sqrt(width)
    return (
        scale * (own_image + arrived[:rows].astype(jnp.float32)),
        scale * (own_text + arrived[rows:].astype(jnp.float32)),
    )


def solution(mesh):
    spec = P(("dp", "group"), None)
    return jax.shard_map(body, mesh=mesh, in_specs=(spec, spec), out_specs=(spec, spec), check_vma=False)
```

time: 57.3 us -> 56.7 us (0.990)
  the two profiles are of different devices: /device:TPU:24 before, /device:TPU:56 now
where the time goes in v2:
time: 56.7 us; the launch traced here: 56.5 us
  Pallas kernels  53.3 us (94%)
  other arithmetic  2.55 us (4%)
  between operations  0.64 us (1%)
    pallas_call x1, Pallas kernels, body(): pl.pallas_call(kernel, out_shape=[jax.ShapeDtypeStruct((rows, width), jnp...  53.3 us
    mul x1, other arithmetic, body(): scale * (own_text + arrived[rows:].astype(jnp.float32))  2.55 us

profile of v2, /device:TPU:56, one launch (start us, length us, event | category | flops | bytes accessed | tf_op | source)
XLA Modules:
  0.0 56.5 jit_solution(13241181909232113676)
XLA Ops:
  0.6 53.3 %shard_map.41 = (f32[128,1152]{1,0:T(8,128)}, f32[128,1152]{1,0:T(8,128)}, bf16[256,1152]{1,0:T(8,128)(2,1)}) custom-call(bf16[128,1152]{1,0:T(8,128)(2,1)} %image_ref.1, bf16[128,1152]{1,0:T(8,128)(2,1)} %text_ref.1), custom_call_target="tpu_custom_call" | custom-call | tf_op jit(solution)/shard_map/pallas_call | solution.py:202
  53.9 2.6 %add_multiply_fusion = (f32[128,1152]{1,0:T(8,128)}, f32[128,1152]{1,0:T(8,128)}) fusion(f32[128,1152]{1,0:T(8,128)} %get-tuple-element.7, bf16[256,1152]{1,0:T(8,128)(2,1)} %get-tuple-element.6, f32[128,1152]{1,0:T(8,128)} %get-tuple-element.5), kind=kLoop, calls=%fused_computation | loop fusion | flops 884736 | bytes 2949120 | tf_op jit(solution)/shard_map/mul | solution.py:222

commit v3 on v2

--- a/solution.py
+++ b/solution.py
@@ -119,7 +119,7 @@
                 else:
                     pl.when(needed)(getattr(c, method))
 
-    pl.when(last)(lambda: each("start", share_up, across_out))
+    pl.when(last)(lambda: each("start", share_up[1:], across_out[1:], across_out[:1], share_up[:1]))
     for pair in imports:
         for c in pair:
             c.start()
@@ -164,14 +164,17 @@
     for s, mine, others in sides:
         fill(s, mine, others, UP, DOWN)
 
-    each("wait_recv", share_up)
-    pl.when(first)(lambda: each("wait_recv", across_in))
-    pl.when(jnp.logical_not(first))(lambda: each("wait_recv", *forward_up))
+    def await_down(kind):
+        this = slice(kind, kind + 1)
+        each("wait_recv", share_up[this])
+        pl.when(first)(lambda: each("wait_recv", across_in[this]))
+        pl.when(jnp.logical_not(first))(lambda: each("wait_recv", *(pair[this] for pair in forward_up)))
 
     width = images.shape[1]
     worked = (DOWN_PARTNER + 1) * ROWS
     stores = [pltpu.make_async_copy(own.at[s], ref, local_sem.at[s]) for s, ref in enumerate((own_image_ref, own_text_ref))]
     for s, mine, others in sides:
+        await_down(1 - s)
         fill(s, mine, others, DOWN, DOWN_PARTNER + 1)
         for t in range(0, width, TILE):
             leaving[block(s), t : t + TILE] = jnp.dot(

time: 56.7 us -> 56.1 us (0.989)
  the two profiles are of different devices: /device:TPU:56 before, /device:TPU:8 now
where the time goes in v3:
time: 56.1 us; the launch traced here: 55.9 us
  Pallas kernels  52.7 us (94%)
  other arithmetic  2.55 us (5%)
  between operations  0.64 us (1%)
    pallas_call x1, Pallas kernels, body(): pl.pallas_call(kernel, out_shape=[jax.ShapeDtypeStruct((rows, width), jnp...  52.7 us
    mul x1, other arithmetic, body(): scale * (own_text + arrived[rows:].astype(jnp.float32))  2.55 us

profile of v3, /device:TPU:8, one launch (start us, length us, event | category | flops | bytes accessed | tf_op | source)
XLA Modules:
  0.0 55.9 jit_solution(3904940032745722313)
XLA Ops:
  0.6 52.7 %shard_map.41 = (f32[128,1152]{1,0:T(8,128)}, f32[128,1152]{1,0:T(8,128)}, bf16[256,1152]{1,0:T(8,128)(2,1)}) custom-call(bf16[128,1152]{1,0:T(8,128)(2,1)} %image_ref.1, bf16[128,1152]{1,0:T(8,128)(2,1)} %text_ref.1), custom_call_target="tpu_custom_call" | custom-call | tf_op jit(solution)/shard_map/pallas_call | solution.py:205
  53.3 2.6 %add_multiply_fusion = (f32[128,1152]{1,0:T(8,128)}, f32[128,1152]{1,0:T(8,128)}) fusion(f32[128,1152]{1,0:T(8,128)} %get-tuple-element.7, bf16[256,1152]{1,0:T(8,128)(2,1)} %get-tuple-element.6, f32[128,1152]{1,0:T(8,128)} %get-tuple-element.5), kind=kLoop, calls=%fused_computation | loop fusion | flops 884736 | bytes 2949120 | tf_op jit(solution)/shard_map/mul | solution.py:225

commit v4 on v3

--- a/solution.py
+++ b/solution.py
@@ -119,7 +119,9 @@
                 else:
                     pl.when(needed)(getattr(c, method))
 
-    pl.when(last)(lambda: each("start", share_up[1:], across_out[1:], across_out[:1], share_up[:1]))
+    pl.when(jnp.logical_and(last, g == 3))(lambda: each("start", across_out[1:], share_up[1:]))
+    pl.when(jnp.logical_and(last, g != 3))(lambda: each("start", share_up[1:], across_out[1:]))
+    pl.when(last)(lambda: each("start", across_out[:1], share_up[:1]))
     for pair in imports:
         for c in pair:
             c.start()

time: 56.1 us -> 57.2 us (1.020)
  Pallas kernels: 52.7 us -> 53.9 us
    pallas_call x1, Pallas kernels: 52.7 us -> 53.9 us  [body(): pl.pallas_call(kernel, out_shape=[jax.ShapeDtypeStruct((rows, width), jnp...]
where the time goes in v4:
time: 57.2 us; the launch traced here: 57 us
  Pallas kernels  53.9 us (94%)
  other arithmetic  2.55 us (4%)
  between operations  0.64 us (1%)
    pallas_call x1, Pallas kernels, body(): pl.pallas_call(kernel, out_shape=[jax.ShapeDtypeStruct((rows, width), jnp...  53.9 us
    mul x1, other arithmetic, body(): scale * (own_text + arrived[rows:].astype(jnp.float32))  2.55 us

profile of v4, /device:TPU:8, one launch (start us, length us, event | category | flops | bytes accessed | tf_op | source)
XLA Modules:
  0.0 57.0 jit_solution(15107412166902622818)
XLA Ops:
  0.6 53.9 %shard_map.41 = (f32[128,1152]{1,0:T(8,128)}, f32[128,1152]{1,0:T(8,128)}, bf16[256,1152]{1,0:T(8,128)(2,1)}) custom-call(bf16[128,1152]{1,0:T(8,128)(2,1)} %image_ref.1, bf16[128,1152]{1,0:T(8,128)(2,1)} %text_ref.1), custom_call_target="tpu_custom_call" | custom-call | tf_op jit(solution)/shard_map/pallas_call | solution.py:207
  54.5 2.6 %add_multiply_fusion = (f32[128,1152]{1,0:T(8,128)}, f32[128,1152]{1,0:T(8,128)}) fusion(f32[128,1152]{1,0:T(8,128)} %get-tuple-element.7, bf16[256,1152]{1,0:T(8,128)(2,1)} %get-tuple-element.6, f32[128,1152]{1,0:T(8,128)} %get-tuple-element.5), kind=kLoop, calls=%fused_computation | loop fusion | flops 884736 | bytes 2949120 | tf_op jit(solution)/shard_map/mul | solution.py:227
